TPU v7x, 32 devices: a whole 2x2x4 slice. The times are simulated.
32 devices in a mesh: grp: 2 (over y), tm: 4 (over z), space: 2 (over x), obs: 2 (over core).
Axes of the slice: x: 2, y: 2, z: 4, core: 2. Of those that a mesh axis runs over, the one named last changes fastest.
Arguments:
- obs_panel: bfloat16 [8192, 768], P(('grp', 'tm', 'space', 'obs')), parts along dimension 0, may hold values from -0.375 to 0.375
- node_index: int32 [8192], P(('grp', 'tm', 'space', 'obs')), parts along dimension 0, may hold values from 0 to 767
- weight: bfloat16 [8192], P(('grp', 'tm', 'space', 'obs')), parts along dimension 0, may hold values from 0.049804688 to 0.5
- residual: bfloat16 [8192], P(('grp', 'tm', 'space', 'obs')), parts along dimension 0, may hold values from -6 to 6
- route_time: int32 [8192], P(('grp', 'tm', 'space', 'obs')), parts along dimension 0, may hold values from 0 to 3, as said below
- spatial_prec: float32 [8, 768, 768], P(('grp', 'tm'), ('space', 'obs')), parts along dimension 0, as said below
- ar_coef: float32 [8], P(('grp', 'tm')), parts along dimension 0, may hold values from 0.5 to 0.85
- prior_rhs: float32 [8, 768], P(('grp', 'tm'), ('space', 'obs')), parts along dimension 0, may hold values from -6 to 6
Outputs:
- reduced_diag: float32 [8, 768, 768], P(('grp', 'tm'), ('space', 'obs')), parts along dimension 0
- fill_block: float32 [8, 768, 768], P(('grp', 'tm'), ('space', 'obs')), parts along dimension 0
- reduced_rhs: float32 [8, 768], P(('grp', 'tm'), ('space', 'obs')), parts along dimension 0
There are 2 independent parts, one for each index of `grp`. A program takes and returns all parts, laid end to end along the dimension named above; each array names one. Nothing has to cross between parts.
Inputs may be any that keep to these rules, and one draw needn't show every extreme that they name: `route_time`: each device's 256 rows name each time block at most 128 times; in every draw one time block receives exactly 128 rows from every device's block of rows. `spatial_prec`: each block is symmetric positive definite.
All inputs are finite; a program needn't handle non-finite values.
Results may differ from a plain program's by a relative error of at most 0.0044.
Values may be sent and summed in bfloat16 or wider, within the bound.
A program may use at most 64 MiB of HBM per device.

v0:
```python
import functools

import jax
import jax.numpy as jnp
from jax import lax
from jax.experimental import pallas as pl
from jax.experimental.pallas import tpu as pltpu
from jax.sharding import PartitionSpec as P

F32 = jnp.float32
BF16 = jnp.bfloat16
NN = (((1,), (0,)), ((), ()))
NT = (((1,), (1,)), ((), ()))
MESH = pl.DeviceIdType.MESH
WIDE = 128
CELLS = ("space", "obs")
GOAL = 2e-3
DOUBLINGS = 12
REFINES = 6


def split(value):
    high = value.astype(BF16)
    return high, (value - high.astype(F32)).astype(BF16)


def mm(left, right, dims=NN):
    return lax.dot_general(left, right, dims, preferred_element_type=F32)


def mm_exact(left, right):
    return lax.dot_general(left, right, NN, precision=lax.Precision.HIGHEST, preferred_element_type=F32)


def solve_kernel(tile, sizes, active_ref, diag_ref, left_ref, right_ref, lows_ref, scales_ref, rhs_ref,
                 out_left, out_right, up_ref, x, e, sq, g, gh, res):
    count = diag_ref.shape[0]
    many = g.shape[0]
    mine = many // 2
    tiles = count // tile
    cell = lax.axis_index("space") * sizes[2] + lax.axis_index("obs")

    def strip(i):
        return pl.ds(pl.multiple_of(i * tile, tile), tile)

    def eye(i):
        row = lax.broadcasted_iota(jnp.int32, (tile, count), 0) + i * tile
        col = lax.broadcasted_iota(jnp.int32, (tile, count), 1)
        return row == col

    def set_rows():
        at = on_diagonal(mine, count, cell)
        here = pl.ds(pl.multiple_of(cell * mine, 16), mine)
        res[:mine, :] = left_ref[here, :].astype(F32) + jnp.where(at, lows_ref[0:1, :], 0.0)
        res[mine:, :] = right_ref[here, :].astype(F32) + jnp.where(at, lows_ref[8:9, :], 0.0)

    def exact_diag(place):
        def body(i, _):
            place[strip(i), :] = diag_ref[strip(i), :].astype(F32) + jnp.where(eye(i), lows_ref[16:17, :], 0.0)
            return 0

        lax.fori_loop(0, tiles, body, 0)

    def sweeps():
        exact_diag(x)
        lane = lax.broadcasted_iota(jnp.int32, (1, count), 1)

        def sweep(k, _):
            pivot_row = x[pl.ds(k, 1), :]
            inv = 1.0 / jnp.sum(jnp.where(lane == k, pivot_row, 0.0), axis=1, keepdims=True)
            row = pivot_row * inv

            def body(i, _):
                part = x[strip(i), :]
                here = lax.broadcasted_iota(jnp.int32, (tile, 1), 0) + i * tile == k
                col = jnp.sum(jnp.where(lane == k, part, 0.0), axis=1, keepdims=True)
                new = jnp.where(lane == k, col * inv, part - col * row)
                x[strip(i), :] = jnp.where(here, jnp.where(lane == k, -inv, row), new)
                return 0

            return lax.fori_loop(0, tiles, body, 0)

        lax.fori_loop(0, count, sweep, 0)
        x[...] = -x[...]

    @pl.when(active_ref[0] == 1)
    def _():
        set_rows()

        def square(i, most):
            part = mm(diag_ref[strip(i), :], diag_ref[...])
            sq[strip(i), :] = part
            return jnp.maximum(most, jnp.max(jnp.sum(jnp.abs(part), axis=1)))

        most = lax.fori_loop(0, tiles, square, jnp.float32(0.0))
        bound = jnp.sqrt(jnp.full((1, 128), most, F32)) * 1.03
        scale = (1.9 / bound)[:, :1]

        def first(i, total):
            diag = diag_ref[strip(i), :].astype(F32) * scale
            one = jnp.where(eye(i), 1.0, 0.0)
            err = one - 2.0 * diag + (scale * scale) * sq[strip(i), :]
            x[strip(i), :] = scale * (2.0 * one - diag)
            e[0, strip(i), :] = err.astype(BF16)
            return total + jnp.sum(err * err)

        total = lax.fori_loop(0, tiles, first, jnp.float32(0.0))

        def more(state):
            step, total = state
            return (total > 2.0) & (step < DOUBLINGS)

        def double(state):
            step, _ = state
            now = lax.rem(step, 2)

            def body(i, total):
                full = e[now]
                part = x[strip(i), :]
                x[strip(i), :] = part + mm(part.astype(BF16), full)
                err = mm(e[now, strip(i), :], full)
                e[1 - now, strip(i), :] = err.astype(BF16)
                return total + jnp.sum(err * err)

            return step + 1, lax.fori_loop(0, tiles, body, jnp.float32(0.0))

        step, _ = lax.while_loop(more, double, (jnp.int32(0), total))
        last = lax.rem(step, 2)

        def finish(i, _):
            part = x[strip(i), :]
            e[1 - last, strip(i), :] = (part + mm(part.astype(BF16), e[last])).astype(BF16)
            return 0

        lax.fori_loop(0, tiles, finish, 0)
        inverse = 1 - last
        begin = mm(res[...].astype(BF16), e[inverse]).astype(BF16)
        gh[...] = begin
        g[...] = begin.astype(F32)

        def again(state):
            step, size = state
            return jnp.logical_not(size <= GOAL * GOAL) & (step < REFINES)

        def refine(state):
            step, _ = state
            done = gh[...]
            rest = res[...] - mm(done, diag_ref[...]) - done.astype(F32) * lows_ref[16:17, :]
            res[...] = rest
            more = mm(rest.astype(BF16), e[inverse]).astype(BF16)
            gh[...] = more
            more = more.astype(F32)
            value = g[...] + more
            g[...] = value
            norm = jnp.sum(value * value, axis=1, keepdims=True) + 1e-30
            return step + 1, jnp.max(jnp.sum(more * more, axis=1, keepdims=True) / norm)

        _, size = lax.while_loop(again, refine, (jnp.int32(0), jnp.float32(1.0)))

        @pl.when(jnp.logical_not(size <= GOAL * GOAL))
        def _():
            sweeps()
            exact_diag(sq)
            g[...] = jnp.zeros_like(g)

            def improve(_, carry):
                set_rows()
                rest = res[...] - mm_exact(g[...], sq[...])
                g[...] += mm_exact(rest, x[...])
                return carry

            lax.fori_loop(0, 3, improve, 0)

        left_scale, right_scale = scales_ref[0:1, 0:1], scales_ref[1:2, 0:1]
        top = lax.broadcasted_iota(jnp.int32, (many, 1), 0) < mine
        value = g[...] * jnp.where(top, left_scale, right_scale)
        high, low = split(value)
        gh[...] = high
        for out, full, scale, at in ((out_left, left_ref, left_scale, 0), (out_right, right_ref, right_scale, 8)):
            out[...] = (mm(gh[...], full[...], NT) + value * lows_ref[at : at + 1, :]) * scale
        rhs_high, rhs_low = split(rhs_ref[...])
        up_ref[...] = mm(rhs_high, gh[...], NT) + mm(rhs_low, gh[...], NT) + mm(rhs_high, low, NT)


def solve(sizes, active, diag, full_left, full_right, lows, scales, rhs):
    count = diag.shape[0]
    many = 2 * (count // (sizes[1] * sizes[2]))
    vmem = pl.BlockSpec(memory_space=pltpu.VMEM)
    tile = 256 if count % 256 == 0 else count
    return pl.pallas_call(
        functools.partial(solve_kernel, tile, sizes),
        out_shape=(
            jax.ShapeDtypeStruct((many, count), F32),
            jax.ShapeDtypeStruct((many, count), F32),
            jax.ShapeDtypeStruct((8, many), F32),
        ),
        in_specs=[pl.BlockSpec(memory_space=pltpu.SMEM)] + [vmem] * 6,
        out_specs=(vmem, vmem, vmem),
        scratch_shapes=[
            pltpu.VMEM((count, count), F32),
            pltpu.VMEM((2, count, count), BF16),
            pltpu.VMEM((count, count), F32),
            pltpu.VMEM((many, count), F32),
            pltpu.VMEM((many, count), BF16),
            pltpu.VMEM((many, count), F32),
        ],
        compiler_params=pltpu.CompilerParams(vmem_limit_bytes=48 * 1024 * 1024),
    )(active.astype(jnp.int32).reshape(1), diag, full_left, full_right, lows, scales, rhs)


def turn(value, by, size):
    return lax.rem(value + (by + size), size)


def send(source, target, send_sem, recv_sem, device):
    return pltpu.make_async_remote_copy(
        src_ref=source, dst_ref=target, send_sem=send_sem, recv_sem=recv_sem, device_id=device, device_id_type=MESH
    )


def greet(devices):
    barrier = pltpu.get_barrier_semaphore()
    for device in devices:
        pl.semaphore_signal(barrier, inc=1, device_id=device, device_id_type=MESH)
    pl.semaphore_wait(barrier, len(devices))


def cell_peers(sp, ob, n_space, n_obs):
    return [
        {"space": turn(sp, k, n_space), "obs": turn(ob, o, n_obs)}
        for k in range(n_space)
        for o in range(n_obs)
        if k or o
    ]


class Spread:
    def __init__(self, buf, sems, which, sizes):
        self.buf, self.n_space, self.n_obs = buf, *sizes
        self.send_sems, self.recv_sems = (sem.at[which] for sem in sems)
        self.sp, self.ob = lax.axis_index("space"), lax.axis_index("obs")
        self.sent = []

    def block(self, k, o):
        return self.buf.at[turn(self.sp, -k, self.n_space) * self.n_obs + turn(self.ob, -o, self.n_obs)]

    def copy(self, k, o, forward):
        source = self.block(k, 0) if forward else self.block(0, 0)
        device = {"obs": turn(self.ob, o, self.n_obs)} if forward else {"space": turn(self.sp, k, self.n_space)}
        made = send(source, source, self.send_sems.at[k, o], self.recv_sems.at[k, o], device)
        made.start()
        self.sent.append(made)

    def arrived(self, k, o):
        place = self.block(k, o)
        send(place, place, self.send_sems.at[k, o], self.recv_sems.at[k, o], {"obs": self.ob}).wait_recv()

    def start(self):
        for k in range(1, self.n_space):
            self.copy(k, 0, False)
        for o in range(1, self.n_obs):
            self.copy(0, o, True)

    def forward(self):
        for k in range(1, self.n_space):
            self.arrived(k, 0)
            for o in range(1, self.n_obs):
                self.copy(k, o, True)

    def finish(self):
        for k in range(self.n_space):
            for o in range(1, self.n_obs):
                self.arrived(k, o)
        for made in self.sent:
            made.wait_send()


def on_diagonal(mine, count, cell):
    row = lax.broadcasted_iota(jnp.int32, (mine, count), 0) + cell * mine
    return row == lax.broadcasted_iota(jnp.int32, (mine, count), 1)


def pack(value, place, at, extra):
    mine, count = value.shape
    high = value.astype(BF16)
    rest = jnp.sum(jnp.where(at, value - high.astype(F32), 0.0), axis=1, keepdims=True)
    lane = lax.broadcasted_iota(jnp.int32, (mine, WIDE), 1)
    beside = jnp.where(lane == 0, rest, 0.0)
    for index, column in enumerate(extra):
        beside = jnp.where(lane == index + 1, column, beside)
    place[:, :count] = high
    place[:, count:] = beside.astype(BF16)


def unpack(place, at):
    count = at.shape[1]
    rest = place[:, count : count + 1].astype(F32)
    low = jnp.where(at, rest, 0.0)
    return place[:, :count].astype(F32) + low, low


def assemble_kernel(sizes, send_ref, prec_ref, coef_ref, vec_ref,
                    diag_rows, diag_full, own_out, next_out, lows_out, scales_out, rhs_out,
                    slabs, arriving, design, weighted, part, part_high, from_mate, half, from_space,
                    own_buf, next_buf, diag_buf, vec_buf,
                    slab_send, slab_recv, prec_sems, mate_send, mate_recv, half_send, half_recv, all_send, all_recv):
    n_times, n_space, n_obs = sizes
    mine, count = prec_ref.shape
    capacity = send_ref.shape[1]
    tm, sp, ob = lax.axis_index("tm"), lax.axis_index("space"), lax.axis_index("obs")
    cell = sp * n_obs + ob
    cells = n_space * n_obs
    at = on_diagonal(mine, count, cell)
    greet([{"tm": turn(tm, k, n_times)} for k in range(1, n_times)] + cell_peers(sp, ob, n_space, n_obs))

    moves = []

    def slab(k):
        there = turn(tm, k, n_times)
        return send(send_ref.at[there], slabs.at[tm], slab_send.at[k], slab_recv.at[k], {"tm": there})

    early, late = list(range(1, n_times, 2)), list(range(2, n_times, 2))
    for parity, first in ((0, early), (1, late)):
        @pl.when(lax.rem(tm, 2) == parity)
        def _():
            for k in first:
                slab(k).start()

    coef = coef_ref[0:1, 0:1]
    coef_high = coef.astype(BF16).astype(F32)
    coef_mid = (coef - coef_high).astype(BF16).astype(F32)
    pack(prec_ref[...], own_buf.at[cell], at, (coef_high, coef_mid, coef - coef_high - coef_mid))
    prec_move = send(own_buf.at[cell], arriving, prec_sems.at[0], prec_sems.at[1], {"tm": turn(tm, -1, n_times)})
    even = lax.rem(tm, 2) == 0

    @pl.when(even)
    def _():
        prec_move.start()

    both = (all_send, all_recv)
    spreads = [Spread(buf, both, i, (n_space, n_obs)) for i, buf in enumerate((own_buf, next_buf, diag_buf, vec_buf))]
    own_spread, next_spread, diag_spread, vec_spread = spreads
    own_spread.start()
    slabs[tm] = send_ref[tm]
    for parity, first, second in ((0, early, late), (1, late, early)):
        @pl.when(lax.rem(tm, 2) == parity)
        def _():
            for k in first:
                slab(k).wait_send()
            if parity == 1:
                prec_move.start()
            for k in second:
                slab(k).start()

    prec_move.wait_recv()
    next_buf[cell] = arriving[...]
    next_spread.start()
    own_spread.forward()
    for k in range(1, n_times):
        place = slabs.at[turn(tm, -k, n_times)]
        send(place, place, slab_send.at[k], slab_recv.at[k], {"tm": tm}).wait_recv()

    grad = jnp.zeros((1, count), F32)
    for t in range(n_times):
        held = slabs[t]
        rows = held[:, :count].astype(F32)
        design[:, t * capacity : (t + 1) * capacity] = rows.T.astype(BF16)
        weighted[t * capacity : (t + 1) * capacity, :] = (held[:, count : count + 1].astype(F32) * rows).astype(BF16)
        grad = grad + jnp.sum(held[:, count + 1 : count + 2].astype(F32) * rows, axis=0, keepdims=True)
    vec_buf[cell] = vec_ref[...] + jnp.broadcast_to(grad, (8, count))
    vec_spread.start()
    for o in range(n_obs):
        for s in range(n_space):
            first = (s * n_obs + o) * mine
            value = mm(design[first : first + mine, :], weighted[...])
            part[o, s] = value
            part_high[o, s] = value.astype(BF16)
    for o in range(1, n_obs):
        mate = turn(ob, o, n_obs)
        move = send(part_high.at[mate], from_mate.at[o], mate_send.at[o], mate_recv.at[o], {"obs": mate})
        move.start()
        moves.append(move)
    next_spread.forward()
    vec_spread.forward()
    for o in range(1, n_obs):
        place = from_mate.at[o]
        send(place, place, mate_send.at[o], mate_recv.at[o], {"obs": ob}).wait_recv()

    def chip_sum(s):
        value = part[ob, s]
        for o in range(1, n_obs):
            value = value + from_mate[o, s].astype(F32)
        return value

    for k in range(1, n_space):
        there = turn(sp, k, n_space)
        half[k] = chip_sum(there).astype(BF16)
        move = send(half.at[k], from_space.at[k], half_send.at[k], half_recv.at[k], {"space": there})
        move.start()
        moves.append(move)
    gram = chip_sum(sp)
    next_rows, _ = unpack(next_buf.at[cell], at)
    three = next_buf[cell, :, count + 1 : count + 4].astype(F32)
    next_coef = jnp.sum(three, axis=1, keepdims=True)
    base = prec_ref[...] + next_coef * next_coef * next_rows + gram
    for k in range(1, n_space):
        place = from_space.at[k]
        send(place, place, half_send.at[k], half_recv.at[k], {"space": sp}).wait_recv()
        base = base + from_space[k].astype(F32)
    diag_rows[...] = base
    pack(base, diag_buf.at[cell], at, ())
    diag_spread.start()
    scales_out[0:1, :] = jnp.broadcast_to(-coef, (1, WIDE))
    scales_out[1:2, :] = jnp.broadcast_to(-next_coef[0:1, :], (1, WIDE))
    scales_out[2:8, :] = jnp.zeros((6, WIDE), F32)
    own_spread.finish()
    next_spread.finish()
    vec_spread.finish()
    total = vec_buf[0]
    for c in range(1, cells):
        total = total + vec_buf[c]
    rhs_out[...] = total
    def emit(at_row, buf, out):
        low_sum = jnp.zeros((1, count), F32)
        for c in range(cells):
            _, low = unpack(buf.at[c], on_diagonal(mine, count, c))
            low_sum = low_sum + jnp.sum(low, axis=0, keepdims=True)
            out[c * mine : (c + 1) * mine, :] = buf[c, :, :count]
        lows_out[at_row : at_row + 8, :] = jnp.broadcast_to(low_sum, (8, count))

    emit(0, own_buf, own_out)
    emit(8, next_buf, next_out)
    diag_spread.forward()
    diag_spread.finish()
    emit(16, diag_buf, diag_full)
    prec_move.wait_send()
    for parity, second in ((0, late), (1, early)):
        @pl.when(lax.rem(tm, 2) == parity)
        def _():
            for k in second:
                slab(k).wait_send()

    for move in moves:
        move.wait_send()


def assemble(sizes, sending, prec, coef, vec):
    n_times, n_space, n_obs = sizes
    mine, count = prec.shape
    capacity = sending.shape[1]
    cells = n_space * n_obs
    slots = n_times * capacity
    vmem = pl.BlockSpec(memory_space=pltpu.VMEM)
    dma = pltpu.SemaphoreType.DMA
    wide = (cells, mine, count + WIDE)
    return pl.pallas_call(
        functools.partial(assemble_kernel, sizes),
        out_shape=(
            jax.ShapeDtypeStruct((mine, count), F32),
            jax.ShapeDtypeStruct((count, count), BF16),
            jax.ShapeDtypeStruct((count, count), BF16),
            jax.ShapeDtypeStruct((count, count), BF16),
            jax.ShapeDtypeStruct((24, count), F32),
            jax.ShapeDtypeStruct((8, WIDE), F32),
            jax.ShapeDtypeStruct((8, count), F32),
        ),
        in_specs=[vmem] * 4,
        out_specs=(vmem,) * 7,
        scratch_shapes=[
            pltpu.VMEM((n_times, capacity, count + WIDE), BF16),
            pltpu.VMEM((mine, count + WIDE), BF16),
            pltpu.VMEM((count, slots), BF16),
            pltpu.VMEM((slots, count), BF16),
            pltpu.VMEM((n_obs, n_space, mine, count), F32),
            pltpu.VMEM((n_obs, n_space, mine, count), BF16),
            pltpu.VMEM((n_obs, n_space, mine, count), BF16),
            pltpu.VMEM((n_space, mine, count), BF16),
            pltpu.VMEM((n_space, mine, count), BF16),
            pltpu.VMEM(wide, BF16),
            pltpu.VMEM(wide, BF16),
            pltpu.VMEM(wide, BF16),
            pltpu.VMEM((cells, 8, count), F32),
            dma((n_times,)),
            dma((n_times,)),
            dma((2,)),
            dma((n_obs,)),
            dma((n_obs,)),
            dma((n_space,)),
            dma((n_space,)),
            dma((4, n_space, n_obs)),
            dma((4, n_space, n_obs)),
        ],
        compiler_params=pltpu.CompilerParams(
            collective_id=0, has_side_effects=True, vmem_limit_bytes=48 * 1024 * 1024
        ),
    )(sending, prec, coef, vec)


def reduce_kernel(sizes, by_left, by_right, up_left, up_right, diag_ref, rhs_ref,
                  diag_rows, diag_full, left_out, right_out, lows_out, rhs_out,
                  to_left, to_right, loss_left, loss_right, in_up_left, in_up_right,
                  left_buf, right_buf, diag_buf, vec_buf,
                  send_sems, recv_sems, all_send, all_recv):
    n_times, n_space, n_obs = sizes
    mine, count = diag_ref.shape
    tm, sp, ob = lax.axis_index("tm"), lax.axis_index("space"), lax.axis_index("obs")
    cell = sp * n_obs + ob
    cells = n_space * n_obs
    left, right = {"tm": turn(tm, -1, n_times)}, {"tm": turn(tm, 1, n_times)}
    greet([left, right] + cell_peers(sp, ob, n_space, n_obs))
    kind = lax.rem(tm, 4)

    def fill_copy(is_left):
        buf, source = (right_buf, to_left) if is_left else (left_buf, to_right)
        which = 3 if is_left else 0
        return send(source.at[1], buf.at[cell], send_sems.at[which], recv_sems.at[which], left if is_left else right)

    def loss_copy(is_left):
        buf, source = (loss_right, to_left) if is_left else (loss_left, to_right)
        which = 4 if is_left else 1
        return send(source.at[0], buf, send_sems.at[which], recv_sems.at[which], left if is_left else right)

    def up_copy(is_left):
        buf, source = (in_up_right, up_left) if is_left else (in_up_left, up_right)
        which = 5 if is_left else 2
        return send(source, buf, send_sems.at[which], recv_sems.at[which], left if is_left else right)

    for middle_left in (False, True):
        @pl.when(kind == (3 if middle_left else 1))
        def _():
            near = to_left if middle_left else to_right
            if middle_left:
                near[1] = (-by_left[mine:, :]).astype(BF16)
            else:
                near[1] = (-by_right[:mine, :]).astype(BF16)
            first = fill_copy(middle_left)
            first.start()
            near[0] = (by_left[:mine, :] if middle_left else by_right[mine:, :]).astype(BF16)
            second = loss_copy(middle_left)
            second.start()
            third = up_copy(middle_left)
            third.start()
            far = to_right if middle_left else to_left
            far[0] = (by_right[mine:, :] if middle_left else by_left[:mine, :]).astype(BF16)
            first.wait_send()
            second.wait_send()
            others = [loss_copy(not middle_left), up_copy(not middle_left)]
            for move in others:
                move.start()
            for move in [third] + others:
                move.wait_send()

    @pl.when(kind != 2)
    def _():
        rhs_out[...] = rhs_ref[...]

    @pl.when(kind % 2 == 1)
    def _():
        diag_rows[...] = diag_ref[...]

    @pl.when(kind == 0)
    def _():
        for is_left in (False, True):
            loss_copy(is_left).wait_recv()
            up_copy(is_left).wait_recv()
        diag_rows[...] = diag_ref[...] - loss_left[...].astype(F32) - loss_right[...].astype(F32)
        rhs_out[...] = rhs_ref[...] - in_up_left[...] - in_up_right[...]

    @pl.when(kind == 2)
    def _():
        both = (all_send, all_recv)
        spreads = [
            Spread(buf, both, i, (n_space, n_obs)) for i, buf in enumerate((left_buf, right_buf, diag_buf, vec_buf))
        ]
        fill_copy(False).wait_recv()
        spreads[0].start()
        fill_copy(True).wait_recv()
        spreads[1].start()
        loss_copy(False).wait_recv()
        loss_copy(True).wait_recv()
        base = diag_ref[...] - loss_left[...].astype(F32) - loss_right[...].astype(F32)
        diag_rows[...] = base
        pack(base, diag_buf.at[cell], on_diagonal(mine, count, cell), ())
        spreads[2].start()
        up_copy(False).wait_recv()
        up_copy(True).wait_recv()
        vec_buf[cell] = in_up_left[...] + in_up_right[...]
        spreads[3].start()
        for spread in spreads:
            spread.forward()
        for spread in spreads:
            spread.finish()
        total = rhs_ref[...]
        low_sum = jnp.zeros((1, count), F32)
        for c in range(cells):
            total = total - vec_buf[c]
            left_out[c * mine : (c + 1) * mine, :] = left_buf[c]
            right_out[c * mine : (c + 1) * mine, :] = right_buf[c]
            _, low = unpack(diag_buf.at[c], on_diagonal(mine, count, c))
            low_sum = low_sum + jnp.sum(low, axis=0, keepdims=True)
            diag_full[c * mine : (c + 1) * mine, :] = diag_buf[c, :, :count]
        lows_out[:16, :] = jnp.zeros((16, count), F32)
        lows_out[16:, :] = jnp.broadcast_to(low_sum, (8, count))
        rhs_out[...] = total


def reduce_level(sizes, by_left, by_right, up_left, up_right, diag, rhs):
    n_times, n_space, n_obs = sizes
    mine, count = diag.shape
    cells = n_space * n_obs
    vmem = pl.BlockSpec(memory_space=pltpu.VMEM)
    dma = pltpu.SemaphoreType.DMA
    return pl.pallas_call(
        functools.partial(reduce_kernel, sizes),
        out_shape=(
            jax.ShapeDtypeStruct((mine, count), F32),
            jax.ShapeDtypeStruct((count, count), BF16),
            jax.ShapeDtypeStruct((count, count), BF16),
            jax.ShapeDtypeStruct((count, count), BF16),
            jax.ShapeDtypeStruct((24, count), F32),
            jax.ShapeDtypeStruct((8, count), F32),
        ),
        in_specs=[vmem] * 6,
        out_specs=(vmem,) * 6,
        scratch_shapes=[
            pltpu.VMEM((2, mine, count), BF16),
            pltpu.VMEM((2, mine, count), BF16),
            pltpu.VMEM((mine, count), BF16),
            pltpu.VMEM((mine, count), BF16),
            pltpu.VMEM((8, count), F32),
            pltpu.VMEM((8, count), F32),
            pltpu.VMEM((cells, mine, count), BF16),
            pltpu.VMEM((cells, mine, count), BF16),
            pltpu.VMEM((cells, mine, count + WIDE), BF16),
            pltpu.VMEM((cells, 8, count), F32),
            dma((6,)),
            dma((6,)),
            dma((4, n_space, n_obs)),
            dma((4, n_space, n_obs)),
        ],
        compiler_params=pltpu.CompilerParams(
            collective_id=1, has_side_effects=True, vmem_limit_bytes=48 * 1024 * 1024
        ),
    )(by_left, by_right, up_left, up_right, diag, rhs)


def last_kernel(n_times, by_left, by_right, up_left, up_right, loss_out, up_out,
                loss_send, loss_recv, up_send, up_recv, sems):
    mine = loss_out.shape[0]
    tm = lax.axis_index("tm")
    ways = [-2] if n_times == 4 else [-2, 2]
    greet([{"tm": turn(tm, way, n_times)} for way in ways])
    kind = lax.rem(tm, 4)

    def copies(i, way):
        device = {"tm": turn(tm, way, n_times)}
        return [
            send(loss_send.at[i], loss_recv.at[i], sems.at[0, i], sems.at[1, i], device),
            send(up_send.at[i], up_recv.at[i], sems.at[2, i], sems.at[3, i], device),
        ]

    @pl.when(kind == 2)
    def _():
        if n_times == 4:
            loss_send[0] = (by_left[:mine, :] + by_right[mine:, :]).astype(BF16)
            up_send[0] = up_left[...] + up_right[...]
        else:
            loss_send[0] = by_left[:mine, :].astype(BF16)
            loss_send[1] = by_right[mine:, :].astype(BF16)
            up_send[0] = up_left[...]
            up_send[1] = up_right[...]
        moves = [move for i, way in enumerate(ways) for move in copies(i, way)]
        for move in moves:
            move.start()
        for move in moves:
            move.wait_send()

    @pl.when(kind == 0)
    def _():
        for i, way in enumerate(ways):
            for move in copies(i, way):
                move.wait_recv()
        loss = loss_recv[0].astype(F32)
        up = up_recv[0]
        for i in range(1, len(ways)):
            loss = loss + loss_recv[i].astype(F32)
            up = up + up_recv[i]
        loss_out[...] = loss
        up_out[...] = up

    @pl.when(kind != 0)
    def _():
        loss_out[...] = jnp.zeros_like(loss_out)
        up_out[...] = jnp.zeros_like(up_out)


def last_level(n_times, by_left, by_right, up_left, up_right):
    many, count = by_left.shape
    mine = many // 2
    ways = 1 if n_times == 4 else 2
    vmem = pl.BlockSpec(memory_space=pltpu.VMEM)
    return pl.pallas_call(
        functools.partial(last_kernel, n_times),
        out_shape=(jax.ShapeDtypeStruct((mine, count), F32), jax.ShapeDtypeStruct((8, count), F32)),
        in_specs=[vmem] * 4,
        out_specs=(vmem, vmem),
        scratch_shapes=[
            pltpu.VMEM((ways, mine, count), BF16),
            pltpu.VMEM((ways, mine, count), BF16),
            pltpu.VMEM((ways, 8, count), F32),
            pltpu.VMEM((ways, 8, count), F32),
            pltpu.SemaphoreType.DMA((4, ways)),
        ],
        compiler_params=pltpu.CompilerParams(
            collective_id=2, has_side_effects=True, vmem_limit_bytes=32 * 1024 * 1024
        ),
    )(by_left, by_right, up_left, up_right)


def route(obs_panel, node_index, weight, residual, route_time, n_times):
    rows_dev, count = obs_panel.shape
    capacity = 2 * rows_dev // n_times
    slots = n_times * capacity
    weighted_res = (weight.astype(F32) * residual.astype(F32)).astype(BF16)
    hits = (node_index[:, None] == lax.iota(jnp.int32, count)[None, :]).astype(F32)
    design = (obs_panel.astype(F32) + hits).astype(BF16)
    marks = route_time[:, None] == lax.iota(jnp.int32, n_times)[None, :]
    below = lax.iota(jnp.int32, rows_dev)[:, None] > lax.iota(jnp.int32, rows_dev)[None, :]
    before = mm(below.astype(BF16), marks.astype(BF16))
    rank = jnp.sum(jnp.where(marks, before, 0.0), axis=1).astype(jnp.int32)
    slot = route_time * capacity + rank
    pick = (lax.iota(jnp.int32, slots)[:, None] == slot[None, :]).astype(BF16)
    extra = jnp.pad(jnp.stack([weight, weighted_res], axis=1), ((0, 0), (0, WIDE - 2)))
    sending = mm(pick, jnp.concatenate([design, extra], axis=1)).astype(BF16)
    return sending.reshape(n_times, capacity, count + WIDE)


def local(sizes, obs_panel, node_index, weight, residual, route_time, spatial_prec, ar_coef, prior_rhs):
    n_times, n_space, n_obs = sizes
    time = lax.axis_index("tm")
    cell = lax.axis_index("space") * n_obs + lax.axis_index("obs")
    _, mine, count = spatial_prec.shape

    def placed(row):
        full = lax.dynamic_update_slice(jnp.zeros((1, count), F32), row, (0, cell * mine))
        return jnp.broadcast_to(full, (8, count))

    def mine_of(full):
        return lax.dynamic_slice(full, (0, cell * mine), (1, mine))[0]

    odd = time % 2 == 1
    middle = time % 4 == 2
    sending = route(obs_panel, node_index, weight, residual, route_time, n_times)
    coef = jnp.broadcast_to(ar_coef[:, None], (8, WIDE))
    diag_one, diag_full, full_left, full_right, lows, scales, rhs_one = assemble(
        sizes, sending, spatial_prec[0], coef, placed(prior_rhs)
    )
    by_left, by_right, up = solve(sizes, odd, diag_full, full_left, full_right, lows, scales, rhs_one)
    fill_one = -by_right[:mine]
    diag_two, diag_full, full_left, full_right, lows, rhs_two = reduce_level(
        sizes, by_left, by_right, placed(up[:1, :mine]), placed(up[:1, mine:]), diag_one, rhs_one
    )
    by_left, by_right, up = solve(
        sizes, middle, diag_full, full_left, full_right, lows, jnp.ones_like(scales), rhs_two
    )
    fill_two = -by_right[:mine]
    loss, back = last_level(n_times, by_left, by_right, placed(up[:1, :mine]), placed(up[:1, mine:]))
    fill = jnp.where(odd, fill_one, jnp.where(middle, fill_two, 0.0))
    return (diag_two - loss)[None], fill[None], (mine_of(rhs_two) - mine_of(back))[None]


def solution(mesh):
    rows = ("grp", "tm", "space", "obs")
    blocks = P(("grp", "tm"), CELLS, None)
    vectors = P(("grp", "tm"), CELLS)
    sizes = tuple(mesh.shape[name] for name in ("tm", "space", "obs"))
    return jax.shard_map(
        functools.partial(local, sizes),
        mesh=mesh,
        in_specs=(P(rows, None), P(rows), P(rows), P(rows), P(rows), blocks, P(("grp", "tm")), vectors),
        out_specs=(blocks, blocks, vectors),
        check_vma=False,
    )
```

profile of v0, /device:TPU:0, one launch (start us, length us, event | category | flops | bytes accessed | tf_op | source)
XLA Modules:
  0.0 164.0 jit_solution(921344283247112145)
XLA Ops:
  0.7 0.9 dynamic_update_slice.20
  1.5 1.2 add_convert_fusion
  2.8 0.0 copy-start.6
  2.8 0.7 multiply_convert_fusion
  3.5 0.7 stack.9
  4.2 0.1 copy.13
  4.3 0.9 fusion
  5.3 0.7 convert_add_fusion
  6.0 0.4 convolution_convert_fusion
  7.1 0.0 copy-done.6
  7.1 56.3 %shard_map.103 = (f32[192,768]{1,0:T(8,128)S(1)}, bf16[768,768]{1,0:T(8,128)(2,1)S(1)}, bf16[768,768]{1,0:T(8,128)(2,1)S(1)}, bf16[768,768]{1,0:T(8,128)(2,1)S(1...) custom-call(bf16[4,128,896]{2,1,0:T(8,128)(2,1)S(1)} %bitcast.15, f32[192,768]{1,0:T(8,128)S(1)} %bitcast.16, ...), custom_call_target="tpu_custom_call" | custom-call | tf_op jit(solution)/shard_map/pallas_call | solution.py:456
  63.4 0.0 copy-start.9
  63.4 0.0 copy-start.11
  63.4 0.2 shard_map.104
  63.7 0.5 copy-done.9
  64.2 0.0 copy-done.11
  64.2 0.0 copy-start
  64.2 1.0 copy-done
  65.2 0.1 fusion.14
  65.3 0.2 dynamic_update_slice.22
  65.5 0.6 broadcast_in_dim.80.up_right
  66.1 0.2 dynamic_update_slice.21
  66.3 0.0 copy-start.10
  66.3 1.1 copy-done.10
  67.4 0.0 copy-start.12
  67.4 0.7 copy-done.12
  68.1 0.0 copy-start.13
  68.1 0.7 copy-done.13
  68.8 47.0 %shard_map.105 = (f32[192,768]{1,0:T(8,128)S(1)}, bf16[768,768]{1,0:T(8,128)(2,1)S(1)}, bf16[768,768]{1,0:T(8,128)(2,1)S(1)}, bf16[768,768]{1,0:T(8,128)(2,1)S(1...) custom-call(f32[384,768]{1,0:T(8,128)S(1)} %get-tuple-element.30.by_left, f32[384,768]{1,0:T(8,128)} %copy-done, ...), custom_call_target="tpu_custom_call" | custom-call | tf_op jit(solution)/shard_map/pallas_call | solution.py:613
  115.8 0.0 copy-start.2
  115.8 1.0 copy-done.2
  116.8 0.0 copy-start.7
  116.8 0.8 copy-done.7
  117.6 0.6 copy-done.14
  118.3 0.6 copy-done.16
  118.9 1.3 copy-done.3
  120.1 0.9 copy-done.15
  121.0 0.7 copy-done.17
  121.8 1.0 copy-done.4
  122.8 0.1 fusion.13
  122.9 0.2 dynamic_update_slice.24
  123.1 0.2 dynamic_update_slice.23
  123.3 1.3 copy-done.5
  124.6 36.8 %shard_map.107 = (f32[192,768]{1,0:T(8,128)S(1)}, f32[8,768]{1,0:T(8,128)S(1)}) custom-call(f32[384,768]{1,0:T(8,128)S(1)} %copy-done.5, f32[384,768]{1,0:T(8,128)S(1)} %get-tuple-element.41.by_right, f32[8,768]{1,0:T(8,128)S(1)} %broadcast_in_dim.83.up_left, f32[8,768]{1,0:T(8,128)S(1)} %broadcast_in_dim.85.up_right), custom_call_target="tpu_custom_call" | custom-call | tf_op jit(solution)/shard_map/pallas_call | solution.py:702
  161.4 1.4 dynamic-slice_subtract_fusion
  162.8 0.0 copy-done.1
  162.8 0.0 copy-done.8
  162.8 1.2 select_bitcast_fusion
  (23 shorter events, 0.1 us)
Async XLA Ops:
  2.8 4.3 %copy-start.6 = (f32[1,192,768]{2,1,0:T(8,128)S(1)}, f32[1,192,768]{2,1,0:T(8,128)}, u32[]{:S(2)}) copy-start(f32[1,192,768]{2,1,0:T(8,128)} %param.13) | copy-start | bytes 1769476
  63.4 0.8 copy-start.9
  63.4 0.8 copy-start.11
  64.2 1.0 copy-start
  66.3 1.1 copy-start.10
  67.4 0.7 copy-start.12
  68.1 0.7 copy-start.13
  115.8 1.0 copy-start.2
  116.8 0.8 copy-start.7
  117.6 0.6 copy-start.14
  118.3 0.6 copy-start.16
  118.9 1.3 copy-start.3
  120.1 0.9 copy-start.15
  121.0 0.7 copy-start.17
  121.8 1.0 copy-start.4
  123.3 1.3 copy-start.5
  124.6 38.2 %copy-start.1 = (f32[384,768]{1,0:T(8,128)S(1)}, f32[384,768]{1,0:T(8,128)}, u32[]{:S(2)}) copy-start(f32[384,768]{1,0:T(8,128)} %copy-done) | copy-start | bytes 3538948
  124.6 38.2 %copy-start.8 = (f32[192,768]{1,0:T(8,128)S(1)}, f32[192,768]{1,0:T(8,128)}, u32[]{:S(2)}) copy-start(f32[192,768]{1,0:T(8,128)} %copy-done.7) | copy-start | bytes 1769476
where the time goes:
time: 165 us; the launch traced here: 164 us
  Pallas kernels  140 us (85%)
  local copies, waits for them, and re-layouts  15.6 us (9%)
  other arithmetic  5.2 us (3%)
    pallas_call x1, Pallas kernels, assemble(): pl.pallas_call(functools.partial(assemble_kernel, sizes), out_shape=(jax....  56.3 us
    pallas_call x1, Pallas kernels, reduce_level(): pl.pallas_call(functools.partial(reduce_kernel, sizes), out_shape=(jax.Sh...  47 us
    pallas_call x1, Pallas kernels, last_level(): pl.pallas_call(functools.partial(last_kernel, n_times), out_shape=(jax.Sh...  36.8 us
    unnamed x37, local copies, waits for them, and re-layouts  12.5 us

commit v1 on v0

--- a/solution.py
+++ b/solution.py
@@ -88,9 +88,9 @@
         set_rows()
 
         def square(i, most):
-            part = mm(diag_ref[strip(i), :], diag_ref[...])
-            sq[strip(i), :] = part
-            return jnp.maximum(most, jnp.max(jnp.sum(jnp.abs(part), axis=1)))
+            part = mm(diag_ref[...], diag_ref[:, strip(i)])
+            sq[:, strip(i)] = part
+            return jnp.maximum(most, jnp.max(jnp.sum(jnp.abs(part), axis=0)))
 
         most = lax.fori_loop(0, tiles, square, jnp.float32(0.0))
         bound = jnp.sqrt(jnp.full((1, 128), most, F32)) * 1.03
@@ -115,11 +115,10 @@
             now = lax.rem(step, 2)
 
             def body(i, total):
-                full = e[now]
-                part = x[strip(i), :]
-                x[strip(i), :] = part + mm(part.astype(BF16), full)
-                err = mm(e[now, strip(i), :], full)
-                e[1 - now, strip(i), :] = err.astype(BF16)
+                part = x[:, strip(i)]
+                x[:, strip(i)] = part + mm(e[now], part.astype(BF16))
+                err = mm(e[now], e[now, :, strip(i)])
+                e[1 - now, :, strip(i)] = err.astype(BF16)
                 return total + jnp.sum(err * err)
 
             return step + 1, lax.fori_loop(0, tiles, body, jnp.float32(0.0))
@@ -128,8 +127,8 @@
         last = lax.rem(step, 2)
 
         def finish(i, _):
-            part = x[strip(i), :]
-            e[1 - last, strip(i), :] = (part + mm(part.astype(BF16), e[last])).astype(BF16)
+            part = x[:, strip(i)]
+            e[1 - last, :, strip(i)] = (part + mm(e[last], part.astype(BF16))).astype(BF16)
             return 0
 
         lax.fori_loop(0, tiles, finish, 0)
@@ -204,7 +203,7 @@
             pltpu.VMEM((many, count), BF16),
             pltpu.VMEM((many, count), F32),
         ],
-        compiler_params=pltpu.CompilerParams(vmem_limit_bytes=48 * 1024 * 1024),
+        compiler_params=pltpu.CompilerParams(vmem_limit_bytes=28 * 1024 * 1024),
     )(active.astype(jnp.int32).reshape(1), diag, full_left, full_right, lows, scales, rhs)
 
 
@@ -299,19 +298,47 @@
     return place[:, :count].astype(F32) + low, low
 
 
-def assemble_kernel(sizes, send_ref, prec_ref, coef_ref, vec_ref,
+def assemble_kernel(sizes, panel_ref, fields_ref, prec_ref, coef_ref, vec_ref,
                     diag_rows, diag_full, own_out, next_out, lows_out, scales_out, rhs_out,
-                    slabs, arriving, design, weighted, part, part_high, from_mate, half, from_space,
+                    send_ref, slabs, arriving, design, weighted, part, part_high, from_mate, half, from_space,
                     own_buf, next_buf, diag_buf, vec_buf,
                     slab_send, slab_recv, prec_sems, mate_send, mate_recv, half_send, half_recv, all_send, all_recv):
     n_times, n_space, n_obs = sizes
     mine, count = prec_ref.shape
+    rows_dev = panel_ref.shape[0]
     capacity = send_ref.shape[1]
+    slots = n_times * capacity
     tm, sp, ob = lax.axis_index("tm"), lax.axis_index("space"), lax.axis_index("obs")
     cell = sp * n_obs + ob
     cells = n_space * n_obs
     at = on_diagonal(mine, count, cell)
-    greet([{"tm": turn(tm, k, n_times)} for k in range(1, n_times)] + cell_peers(sp, ob, n_space, n_obs))
+    greeted = [{"tm": turn(tm, k, n_times)} for k in range(1, n_times)] + cell_peers(sp, ob, n_space, n_obs)
+    barrier = pltpu.get_barrier_semaphore()
+    for device in greeted:
+        pl.semaphore_signal(barrier, inc=1, device_id=device, device_id_type=MESH)
+
+    node, route = fields_ref[0:1, :], fields_ref[1:2, :]
+    weight, residual = fields_ref[2:3, :], fields_ref[3:4, :]
+    weighted_res = (weight * residual).astype(BF16).astype(F32)
+    groups = max(8, n_times)
+    marks = lax.broadcasted_iota(jnp.int32, (groups, rows_dev), 0).astype(F32) == route
+    earlier = lax.broadcasted_iota(jnp.int32, (rows_dev, rows_dev), 0) < lax.broadcasted_iota(
+        jnp.int32, (rows_dev, rows_dev), 1
+    )
+    before = mm(jnp.where(marks, 1.0, 0.0).astype(BF16), jnp.where(earlier, 1.0, 0.0).astype(BF16))
+    slot = route * capacity + jnp.sum(jnp.where(marks, before, 0.0), axis=0, keepdims=True)
+    here = lax.broadcasted_iota(jnp.int32, (slots, rows_dev), 0).astype(F32) == slot
+    pick = jnp.where(here, 1.0, 0.0).astype(BF16)
+    hits = lax.broadcasted_iota(jnp.int32, (count, rows_dev), 0).astype(F32) == node
+    packed = (mm(pick, panel_ref[...]) + mm(pick, jnp.where(hits, 1.0, 0.0).astype(BF16), NT)).astype(BF16)
+    slot_weight = jnp.sum(jnp.where(here, weight, 0.0), axis=1, keepdims=True)
+    slot_res = jnp.sum(jnp.where(here, weighted_res, 0.0), axis=1, keepdims=True)
+    lane = lax.broadcasted_iota(jnp.int32, (slots, WIDE), 1)
+    beside = jnp.where(lane == 0, slot_weight, jnp.where(lane == 1, slot_res, 0.0)).astype(BF16)
+    for t in range(n_times):
+        send_ref[t, :, :count] = packed[t * capacity : (t + 1) * capacity, :]
+        send_ref[t, :, count:] = beside[t * capacity : (t + 1) * capacity, :]
+    pl.semaphore_wait(barrier, len(greeted))
 
     moves = []
 
@@ -444,10 +471,10 @@
         move.wait_send()
 
 
-def assemble(sizes, sending, prec, coef, vec):
+def assemble(sizes, panel, fields, prec, coef, vec):
     n_times, n_space, n_obs = sizes
     mine, count = prec.shape
-    capacity = sending.shape[1]
+    capacity = 2 * panel.shape[0] // n_times
     cells = n_space * n_obs
     slots = n_times * capacity
     vmem = pl.BlockSpec(memory_space=pltpu.VMEM)
@@ -464,9 +491,10 @@
             jax.ShapeDtypeStruct((8, WIDE), F32),
             jax.ShapeDtypeStruct((8, count), F32),
         ),
-        in_specs=[vmem] * 4,
+        in_specs=[vmem] * 5,
         out_specs=(vmem,) * 7,
         scratch_shapes=[
+            pltpu.VMEM((n_times, capacity, count + WIDE), BF16),
             pltpu.VMEM((n_times, capacity, count + WIDE), BF16),
             pltpu.VMEM((mine, count + WIDE), BF16),
             pltpu.VMEM((count, slots), BF16),
@@ -491,9 +519,9 @@
             dma((4, n_space, n_obs)),
         ],
         compiler_params=pltpu.CompilerParams(
-            collective_id=0, has_side_effects=True, vmem_limit_bytes=48 * 1024 * 1024
+            collective_id=0, has_side_effects=True, vmem_limit_bytes=32 * 1024 * 1024
         ),
-    )(sending, prec, coef, vec)
+    )(panel, fields, prec, coef, vec)
 
 
 def reduce_kernel(sizes, by_left, by_right, up_left, up_right, diag_ref, rhs_ref,
@@ -639,7 +667,7 @@
             dma((4, n_space, n_obs)),
         ],
         compiler_params=pltpu.CompilerParams(
-            collective_id=1, has_side_effects=True, vmem_limit_bytes=48 * 1024 * 1024
+            collective_id=1, has_side_effects=True, vmem_limit_bytes=20 * 1024 * 1024
         ),
     )(by_left, by_right, up_left, up_right, diag, rhs)
 
@@ -712,27 +740,9 @@
             pltpu.SemaphoreType.DMA((4, ways)),
         ],
         compiler_params=pltpu.CompilerParams(
-            collective_id=2, has_side_effects=True, vmem_limit_bytes=32 * 1024 * 1024
+            collective_id=2, has_side_effects=True, vmem_limit_bytes=12 * 1024 * 1024
         ),
     )(by_left, by_right, up_left, up_right)
-
-
-def route(obs_panel, node_index, weight, residual, route_time, n_times):
-    rows_dev, count = obs_panel.shape
-    capacity = 2 * rows_dev // n_times
-    slots = n_times * capacity
-    weighted_res = (weight.astype(F32) * residual.astype(F32)).astype(BF16)
-    hits = (node_index[:, None] == lax.iota(jnp.int32, count)[None, :]).astype(F32)
-    design = (obs_panel.astype(F32) + hits).astype(BF16)
-    marks = route_time[:, None] == lax.iota(jnp.int32, n_times)[None, :]
-    below = lax.iota(jnp.int32, rows_dev)[:, None] > lax.iota(jnp.int32, rows_dev)[None, :]
-    before = mm(below.astype(BF16), marks.astype(BF16))
-    rank = jnp.sum(jnp.where(marks, before, 0.0), axis=1).astype(jnp.int32)
-    slot = route_time * capacity + rank
-    pick = (lax.iota(jnp.int32, slots)[:, None] == slot[None, :]).astype(BF16)
-    extra = jnp.pad(jnp.stack([weight, weighted_res], axis=1), ((0, 0), (0, WIDE - 2)))
-    sending = mm(pick, jnp.concatenate([design, extra], axis=1)).astype(BF16)
-    return sending.reshape(n_times, capacity, count + WIDE)
 
 
 def local(sizes, obs_panel, node_index, weight, residual, route_time, spatial_prec, ar_coef, prior_rhs):
@@ -750,10 +760,11 @@
 
     odd = time % 2 == 1
     middle = time % 4 == 2
-    sending = route(obs_panel, node_index, weight, residual, route_time, n_times)
+    fields = jnp.stack([value.astype(F32) for value in (node_index, route_time, weight, residual)])
+    fields = jnp.concatenate([fields, jnp.zeros_like(fields)], axis=0)
     coef = jnp.broadcast_to(ar_coef[:, None], (8, WIDE))
     diag_one, diag_full, full_left, full_right, lows, scales, rhs_one = assemble(
-        sizes, sending, spatial_prec[0], coef, placed(prior_rhs)
+        sizes, obs_panel, fields, spatial_prec[0], coef, placed(prior_rhs)
     )
     by_left, by_right, up = solve(sizes, odd, diag_full, full_left, full_right, lows, scales, rhs_one)
     fill_one = -by_right[:mine]

time: 165 us -> 162 us (0.982)
  Pallas kernels: 140 us -> 136 us
  local copies, waits for them, and re-layouts: 15.6 us -> 18.2 us
    unnamed x37 -> x38, local copies, waits for them, and re-layouts: 12.5 us -> 15.8 us
    pallas_call x1, Pallas kernels: 47 us -> 44 us  [reduce_level(): pl.pallas_call(functools.partial(reduce_kernel, sizes), out_shape=(jax.Sh...]
where the time goes in v1:
time: 162 us; the launch traced here: 161 us
  Pallas kernels  136 us (84%)
  local copies, waits for them, and re-layouts  18.2 us (11%)
  other arithmetic  5.19 us (3%)
    pallas_call x1, Pallas kernels, assemble(): pl.pallas_call(functools.partial(assemble_kernel, sizes), out_shape=(jax....  56.5 us
    pallas_call x1, Pallas kernels, reduce_level(): pl.pallas_call(functools.partial(reduce_kernel, sizes), out_shape=(jax.Sh...  44 us
    pallas_call x1, Pallas kernels, last_level(): pl.pallas_call(functools.partial(last_kernel, n_times), out_shape=(jax.Sh...  35.6 us
    unnamed x38, local copies, waits for them, and re-layouts  15.8 us

profile of v1, /device:TPU:0, one launch (start us, length us, event | category | flops | bytes accessed | tf_op | source)
XLA Modules:
  0.0 161.2 jit_solution(7228231205407822719)
XLA Ops:
  0.7 0.9 dynamic_update_slice.20
  1.5 0.7 convert_element_type.4
  2.2 0.7 convert_element_type.5
  2.9 0.7 stack.24
  3.6 0.7 stack.25
  4.9 0.0 copy-start.6
  4.9 1.1 copy-done.6
  6.0 0.0 copy-start.11
  6.0 1.0 copy-done.11
  7.0 56.5 %shard_map.103 = (f32[192,768]{1,0:T(8,128)S(1)}, bf16[768,768]{1,0:T(8,128)(2,1)S(1)}, bf16[768,768]{1,0:T(8,128)(2,1)S(1)}, bf16[768,768]{1,0:T(8,128)(2,1)S(1...) custom-call(bf16[256,768]{1,0:T(8,128)(2,1)S(1)} %copy-done.11, ...), custom_call_target="tpu_custom_call" | custom-call | tf_op jit(solution)/shard_map/pallas_call | solution.py:483
  63.5 0.0 copy-start.9
  63.5 0.0 copy-start.12
  63.5 0.2 shard_map.104
  63.8 0.5 copy-done.9
  64.3 0.0 copy-done.12
  64.3 0.1 fusion.1
  64.4 0.2 dynamic_update_slice.22
  64.6 0.6 broadcast_in_dim.71.up_right
  65.2 0.2 dynamic_update_slice.21
  65.4 0.0 copy-start.10
  65.4 1.1 copy-done.10
  66.4 0.0 copy-start.13
  66.4 0.7 copy-done.13
  67.2 0.0 copy-start.14
  67.2 0.7 copy-done.14
  67.9 44.0 %shard_map.105 = (f32[192,768]{1,0:T(8,128)S(1)}, bf16[768,768]{1,0:T(8,128)(2,1)S(1)}, bf16[768,768]{1,0:T(8,128)(2,1)S(1)}, bf16[768,768]{1,0:T(8,128)(2,1)S(1...) custom-call(f32[384,768]{1,0:T(8,128)S(1)} %get-tuple-element.30.by_left, f32[384,768]{1,0:T(8,128)S(1)} %get-tuple-element.31.by_right, ...), custom_call_target="tpu_custom_call" | custom-call | tf_op jit(solution)/shard_map/pallas_call | solution.py:641
  112.0 0.0 copy-start
  112.0 1.0 copy-done
  113.0 0.0 copy-start.2
  113.0 1.0 copy-done.2
  114.0 0.0 copy-start.7
  114.0 0.8 copy-done.7
  114.9 0.0 copy-start.15
  114.9 0.6 copy-done.15
  115.5 0.6 copy-done.17
  116.1 1.3 copy-done.1
  117.4 1.3 copy-done.3
  118.6 0.9 copy-done.16
  119.5 0.7 copy-done.18
  120.3 1.1 copy-done.4
  121.3 0.1 fusion
  121.4 0.2 dynamic_update_slice.24
  121.6 0.2 dynamic_update_slice.23
  121.8 1.3 copy-done.5
  123.1 35.6 %shard_map.107 = (f32[192,768]{1,0:T(8,128)S(1)}, f32[8,768]{1,0:T(8,128)S(1)}) custom-call(f32[384,768]{1,0:T(8,128)S(1)} %copy-done.5, f32[384,768]{1,0:T(8,128)S(1)} %get-tuple-element.41.by_right, f32[8,768]{1,0:T(8,128)S(1)} %broadcast_in_dim.74.up_left, f32[8,768]{1,0:T(8,128)S(1)} %broadcast_in_dim.76.up_right), custom_call_target="tpu_custom_call" | custom-call | tf_op jit(solution)/shard_map/pallas_call | solution.py:730
  158.7 1.4 dynamic-slice_subtract_fusion
  160.0 0.0 copy-done.8
  160.0 1.2 select_bitcast_fusion
  (22 shorter events, 0.1 us)
Async XLA Ops:
  4.9 1.1 copy-start.6
  6.0 1.0 copy-start.11
  63.5 0.8 copy-start.9
  63.5 0.8 copy-start.12
  65.4 1.1 copy-start.10
  66.4 0.7 copy-start.13
  67.2 0.7 copy-start.14
  112.0 1.1 copy-start
  113.0 1.0 copy-start.2
  114.0 0.8 copy-start.7
  114.9 0.6 copy-start.15
  115.5 0.6 copy-start.17
  116.1 1.3 copy-start.1
  117.4 1.3 copy-start.3
  118.6 0.9 copy-start.16
  119.5 0.7 copy-start.18
  120.3 1.1 copy-start.4
  121.8 1.3 copy-start.5
  123.1 37.0 %copy-start.8 = (f32[192,768]{1,0:T(8,128)S(1)}, f32[192,768]{1,0:T(8,128)}, u32[]{:S(2)}) copy-start(f32[192,768]{1,0:T(8,128)} %copy-done.7) | copy-start | bytes 1769476

commit v2 on v1

--- a/solution.py
+++ b/solution.py
@@ -32,7 +32,7 @@
     return lax.dot_general(left, right, NN, precision=lax.Precision.HIGHEST, preferred_element_type=F32)
 
 
-def solve_kernel(tile, sizes, active_ref, diag_ref, left_ref, right_ref, lows_ref, scales_ref, rhs_ref,
+def solve_kernel(tile, sizes, active_ref, diag_ref, left_ref, right_ref, lows_ref, scales_ref,
                  out_left, out_right, up_ref, x, e, sq, g, gh, res):
     count = diag_ref.shape[0]
     many = g.shape[0]
@@ -177,11 +177,11 @@
         gh[...] = high
         for out, full, scale, at in ((out_left, left_ref, left_scale, 0), (out_right, right_ref, right_scale, 8)):
             out[...] = (mm(gh[...], full[...], NT) + value * lows_ref[at : at + 1, :]) * scale
-        rhs_high, rhs_low = split(rhs_ref[...])
+        rhs_high, rhs_low = split(lows_ref[24:, :])
         up_ref[...] = mm(rhs_high, gh[...], NT) + mm(rhs_low, gh[...], NT) + mm(rhs_high, low, NT)
 
 
-def solve(sizes, active, diag, full_left, full_right, lows, scales, rhs):
+def solve(sizes, active, diag, full_left, full_right, lows, scales):
     count = diag.shape[0]
     many = 2 * (count // (sizes[1] * sizes[2]))
     vmem = pl.BlockSpec(memory_space=pltpu.VMEM)
@@ -193,7 +193,7 @@
             jax.ShapeDtypeStruct((many, count), F32),
             jax.ShapeDtypeStruct((8, many), F32),
         ),
-        in_specs=[pl.BlockSpec(memory_space=pltpu.SMEM)] + [vmem] * 6,
+        in_specs=[pl.BlockSpec(memory_space=pltpu.SMEM)] + [vmem] * 5,
         out_specs=(vmem, vmem, vmem),
         scratch_shapes=[
             pltpu.VMEM((count, count), F32),
@@ -204,7 +204,7 @@
             pltpu.VMEM((many, count), F32),
         ],
         compiler_params=pltpu.CompilerParams(vmem_limit_bytes=28 * 1024 * 1024),
-    )(active.astype(jnp.int32).reshape(1), diag, full_left, full_right, lows, scales, rhs)
+    )(active.astype(jnp.int32).reshape(1), diag, full_left, full_right, lows, scales)
 
 
 def turn(value, by, size):
@@ -299,7 +299,7 @@
 
 
 def assemble_kernel(sizes, panel_ref, fields_ref, prec_ref, coef_ref, vec_ref,
-                    diag_rows, diag_full, own_out, next_out, lows_out, scales_out, rhs_out,
+                    diag_rows, diag_full, own_out, next_out, lows_out, scales_out,
                     send_ref, slabs, arriving, design, weighted, part, part_high, from_mate, half, from_space,
                     own_buf, next_buf, diag_buf, vec_buf,
                     slab_send, slab_recv, prec_sems, mate_send, mate_recv, half_send, half_recv, all_send, all_recv):
@@ -446,7 +446,7 @@
     total = vec_buf[0]
     for c in range(1, cells):
         total = total + vec_buf[c]
-    rhs_out[...] = total
+    lows_out[24:, :] = total
     def emit(at_row, buf, out):
         low_sum = jnp.zeros((1, count), F32)
         for c in range(cells):
@@ -487,12 +487,11 @@
             jax.ShapeDtypeStruct((count, count), BF16),
             jax.ShapeDtypeStruct((count, count), BF16),
             jax.ShapeDtypeStruct((count, count), BF16),
-            jax.ShapeDtypeStruct((24, count), F32),
+            jax.ShapeDtypeStruct((32, count), F32),
             jax.ShapeDtypeStruct((8, WIDE), F32),
-            jax.ShapeDtypeStruct((8, count), F32),
         ),
         in_specs=[vmem] * 5,
-        out_specs=(vmem,) * 7,
+        out_specs=(vmem,) * 6,
         scratch_shapes=[
             pltpu.VMEM((n_times, capacity, count + WIDE), BF16),
             pltpu.VMEM((n_times, capacity, count + WIDE), BF16),
@@ -525,7 +524,7 @@
 
 
 def reduce_kernel(sizes, by_left, by_right, up_left, up_right, diag_ref, rhs_ref,
-                  diag_rows, diag_full, left_out, right_out, lows_out, rhs_out,
+                  diag_rows, diag_full, left_out, right_out, lows_out,
                   to_left, to_right, loss_left, loss_right, in_up_left, in_up_right,
                   left_buf, right_buf, diag_buf, vec_buf,
                   send_sems, recv_sems, all_send, all_recv):
@@ -580,7 +579,7 @@
 
     @pl.when(kind != 2)
     def _():
-        rhs_out[...] = rhs_ref[...]
+        lows_out[24:, :] = rhs_ref[24:, :]
 
     @pl.when(kind % 2 == 1)
     def _():
@@ -592,7 +591,7 @@
             loss_copy(is_left).wait_recv()
             up_copy(is_left).wait_recv()
         diag_rows[...] = diag_ref[...] - loss_left[...].astype(F32) - loss_right[...].astype(F32)
-        rhs_out[...] = rhs_ref[...] - in_up_left[...] - in_up_right[...]
+        lows_out[24:, :] = rhs_ref[24:, :] - in_up_left[...] - in_up_right[...]
 
     @pl.when(kind == 2)
     def _():
@@ -618,7 +617,7 @@
             spread.forward()
         for spread in spreads:
             spread.finish()
-        total = rhs_ref[...]
+        total = rhs_ref[24:, :]
         low_sum = jnp.zeros((1, count), F32)
         for c in range(cells):
             total = total - vec_buf[c]
@@ -628,8 +627,8 @@
             low_sum = low_sum + jnp.sum(low, axis=0, keepdims=True)
             diag_full[c * mine : (c + 1) * mine, :] = diag_buf[c, :, :count]
         lows_out[:16, :] = jnp.zeros((16, count), F32)
-        lows_out[16:, :] = jnp.broadcast_to(low_sum, (8, count))
-        rhs_out[...] = total
+        lows_out[16:24, :] = jnp.broadcast_to(low_sum, (8, count))
+        lows_out[24:, :] = total
 
 
 def reduce_level(sizes, by_left, by_right, up_left, up_right, diag, rhs):
@@ -645,11 +644,10 @@
             jax.ShapeDtypeStruct((count, count), BF16),
             jax.ShapeDtypeStruct((count, count), BF16),
             jax.ShapeDtypeStruct((count, count), BF16),
-            jax.ShapeDtypeStruct((24, count), F32),
-            jax.ShapeDtypeStruct((8, count), F32),
+            jax.ShapeDtypeStruct((32, count), F32),
         ),
         in_specs=[vmem] * 6,
-        out_specs=(vmem,) * 6,
+        out_specs=(vmem,) * 5,
         scratch_shapes=[
             pltpu.VMEM((2, mine, count), BF16),
             pltpu.VMEM((2, mine, count), BF16),
@@ -763,21 +761,21 @@
     fields = jnp.stack([value.astype(F32) for value in (node_index, route_time, weight, residual)])
     fields = jnp.concatenate([fields, jnp.zeros_like(fields)], axis=0)
     coef = jnp.broadcast_to(ar_coef[:, None], (8, WIDE))
-    diag_one, diag_full, full_left, full_right, lows, scales, rhs_one = assemble(
+    diag_one, diag_full, full_left, full_right, lows, scales = assemble(
         sizes, obs_panel, fields, spatial_prec[0], coef, placed(prior_rhs)
     )
-    by_left, by_right, up = solve(sizes, odd, diag_full, full_left, full_right, lows, scales, rhs_one)
+    by_left, by_right, up = solve(sizes, odd, diag_full, full_left, full_right, lows, scales)
     fill_one = -by_right[:mine]
-    diag_two, diag_full, full_left, full_right, lows, rhs_two = reduce_level(
-        sizes, by_left, by_right, placed(up[:1, :mine]), placed(up[:1, mine:]), diag_one, rhs_one
+    diag_two, diag_full, full_left, full_right, lows = reduce_level(
+        sizes, by_left, by_right, placed(up[:1, :mine]), placed(up[:1, mine:]), diag_one, lows
     )
     by_left, by_right, up = solve(
-        sizes, middle, diag_full, full_left, full_right, lows, jnp.ones_like(scales), rhs_two
+        sizes, middle, diag_full, full_left, full_right, lows, jnp.ones_like(scales)
     )
     fill_two = -by_right[:mine]
     loss, back = last_level(n_times, by_left, by_right, placed(up[:1, :mine]), placed(up[:1, mine:]))
     fill = jnp.where(odd, fill_one, jnp.where(middle, fill_two, 0.0))
-    return (diag_two - loss)[None], fill[None], (mine_of(rhs_two) - mine_of(back))[None]
+    return (diag_two - loss)[None], fill[None], (mine_of(lows[24:]) - mine_of(back))[None]
 
 
 def solution(mesh):

time: 162 us -> 162 us (level)
  local copies, waits for them, and re-layouts: 18.2 us -> 20.1 us
where the time goes in v2:
time: 162 us
  Pallas kernels  136 us (84%)
  local copies, waits for them, and re-layouts  20.1 us (12%)
  other arithmetic  4.48 us (3%)
    pallas_call x1, Pallas kernels, assemble(): pl.pallas_call(functools.partial(assemble_kernel, sizes), out_shape=(jax....  56.5 us
    pallas_call x1, Pallas kernels, reduce_level(): pl.pallas_call(functools.partial(reduce_kernel, sizes), out_shape=(jax.Sh...  44 us
    pallas_call x1, Pallas kernels, last_level(): pl.pallas_call(functools.partial(last_kernel, n_times), out_shape=(jax.Sh...  35.6 us
    unnamed x38, local copies, waits for them, and re-layouts  16.9 us

profile of v2, /device:TPU:0, one launch (start us, length us, event | category | flops | bytes accessed | tf_op | source)
XLA Modules:
  0.0 162.4 jit_solution(1371718931532960776)
XLA Ops:
  0.7 0.9 dynamic_update_slice.20
  1.5 0.7 convert_element_type.4
  2.2 0.7 convert_element_type.5
  2.9 0.7 stack.24
  3.6 0.7 stack.25
  4.9 0.0 copy-start.8
  4.9 1.1 copy-done.8
  6.0 0.0 copy-start.15
  6.0 1.0 copy-done.15
  7.0 56.5 %shard_map.103 = (f32[192,768]{1,0:T(8,128)S(1)}, bf16[768,768]{1,0:T(8,128)(2,1)S(1)}, bf16[768,768]{1,0:T(8,128)(2,1)S(1)}, bf16[768,768]{1,0:T(8,128)(2,1)S(1...) custom-call(bf16[256,768]{1,0:T(8,128)(2,1)S(1)} %copy-done.15, f32[8,256]{1,0:T(8,128)S(1)} %concatenate.3.fields_ref, ...), custom_call_target="tpu_custom_call" | custom-call | tf_op jit(solution)/shard_map/pallas_call | solution.py:483
  63.5 0.0 copy-start.11
  63.5 0.0 copy-start.13
  63.5 0.2 shard_map.104
  63.8 0.5 copy-done.11
  64.3 0.0 copy-done.13
  64.3 0.0 copy-start.4
  64.3 1.1 copy-done.4
  65.4 0.1 fusion.1
  65.4 0.2 dynamic_update_slice.22
  65.6 0.6 broadcast_in_dim.71.up_right
  66.2 0.2 dynamic_update_slice.21
  66.4 0.0 copy-start.5
  66.4 1.3 copy-done.5
  67.7 0.0 copy-start.12
  67.7 1.1 copy-done.12
  68.8 0.0 copy-start.14
  68.8 0.9 copy-done.14
  69.7 0.0 copy-start.18
  69.7 0.7 copy-done.18
  70.4 44.0 %shard_map.105 = (f32[192,768]{1,0:T(8,128)S(1)}, bf16[768,768]{1,0:T(8,128)(2,1)S(1)}, bf16[768,768]{1,0:T(8,128)(2,1)S(1)}, bf16[768,768]{1,0:T(8,128)(2,1)S(1)}, f32[32,768]{1,0:T(8,128)S(1)}) custom-call(f32[384,768]{1,0:T(8,128)S(1)} %copy-done.5, f32[384,768]{1,0:T(8,128)S(1)} %get-tuple-element.28.by_right, f32[8,768]{1,0:T(8,128)S(1)} %broadcast_in_dim.69.up_left, ...), custom_call_target="tpu_custom_call" | custom-call | tf_op jit(solution)/shard_map/pallas_call | solution.py:640
  114.4 0.0 copy-start
  114.4 1.0 copy-done
  115.5 1.0 copy-done.2
  116.5 0.8 copy-done.9
  117.3 0.6 copy-done.16
  118.0 1.3 copy-done.1
  119.2 1.3 copy-done.3
  120.5 0.9 copy-done.17
  121.4 1.1 copy-done.6
  122.5 0.1 fusion
  122.5 0.2 dynamic_update_slice.24
  122.7 0.2 dynamic_update_slice.23
  123.0 1.3 copy-done.7
  124.2 35.6 %shard_map.107 = (f32[192,768]{1,0:T(8,128)S(1)}, f32[8,768]{1,0:T(8,128)S(1)}) custom-call(f32[384,768]{1,0:T(8,128)S(1)} %copy-done.7, f32[384,768]{1,0:T(8,128)S(1)} %get-tuple-element.37.by_right, f32[8,768]{1,0:T(8,128)S(1)} %broadcast_in_dim.74.up_left, f32[8,768]{1,0:T(8,128)S(1)} %broadcast_in_dim.76.up_right), custom_call_target="tpu_custom_call" | custom-call | tf_op jit(solution)/shard_map/pallas_call | solution.py:728
  159.8 0.7 slice.27
  160.6 0.6 dynamic-slice_subtract_fusion
  161.2 0.0 copy-done.10
  161.2 1.2 select_bitcast_fusion
  (23 shorter events, 0.1 us)
Async XLA Ops:
  4.9 1.1 copy-start.8
  6.0 1.0 copy-start.15
  63.5 0.8 copy-start.11
  63.5 0.8 copy-start.13
  64.3 1.1 copy-start.4
  66.4 1.3 copy-start.5
  67.7 1.1 copy-start.12
  68.8 0.9 copy-start.14
  69.7 0.7 copy-start.18
  114.4 1.1 copy-start
  115.5 1.0 copy-start.2
  116.5 0.8 copy-start.9
  117.3 0.6 copy-start.16
  118.0 1.3 copy-start.1
  119.2 1.3 copy-start.3
  120.5 0.9 copy-start.17
  121.4 1.1 copy-start.6
  123.0 1.3 copy-start.7
  124.2 37.0 %copy-start.10 = (f32[192,768]{1,0:T(8,128)S(1)}, f32[192,768]{1,0:T(8,128)}, u32[]{:S(2)}) copy-start(f32[192,768]{1,0:T(8,128)} %copy-done.9) | copy-start | bytes 1769476
